TPU v7x, 512 devices: a whole 4x4x16 slice. The times are simulated.
512 devices in a mesh: row: 32 (over z, core), col: 16 (over y, x).
Axes of the slice: x: 4, y: 4, z: 16, core: 2. Of those that a mesh axis runs over, the one named last changes fastest.
Arguments:
- solved: float32 [2, 32768, 512], P(None, 'row'), may hold values from -6 to 6
- upper_cols: float32 [2, 2, 1024, 32768], P(None, None, 'col', 'row'), may hold values from -0.0234375 to 0.0234375
- coupling: float32 [2, 1024, 1024], P(None, 'col', 'row'), may hold values from -0.125 to 0.125
- inverse_diag: float32 [2, 2, 1024, 1024], P(None, None, 'row', 'col'), may hold values from -0.1875 to 0.1875
- right_side: float32 [2, 2, 1024, 512], P(None, None, 'col'), may hold values from -6 to 6
Outputs:
- answers: float32 [2, 2, 1024, 512], P(None, None, 'row')
All inputs are finite; a program needn't handle non-finite values.
Results may differ from a plain program's by a relative error of at most 0.000082.
Values sent between devices are 32-bit elements; how exact they have to be, the bound alone decides.
A program may use at most 64 MiB of HBM per device.

v0:
```python
import jax
import jax.numpy as jnp
from jax import lax
from jax.sharding import PartitionSpec as P

HIGHEST = lax.Precision.HIGHEST


def padded_to(lines, size):
    spare = -lines.shape[0] % size
    if not spare:
        return lines
    return jnp.concatenate([lines, jnp.zeros((spare, *lines.shape[1:]), lines.dtype)])


def sent_to_all(shard, axis):
    size = lax.axis_size(axis)
    return lax.all_to_all(
        jnp.broadcast_to(shard[None], (size, *shard.shape)), axis, 0, 0, tiled=True
    )


def joined_along(parts, dim):
    parts = jnp.moveaxis(parts, 0, dim)
    lengths = parts.shape
    return parts.reshape(*lengths[:dim], lengths[dim] * lengths[dim + 1], *lengths[dim + 2 :])


def gathered_copies(shard, axis, dim):
    parts = sent_to_all(shard, axis)
    return joined_along(parts, dim)


def cut_along(shard, dim, size):
    before, after = (shard.shape[:dim], shard.shape[dim + 1 :])
    return jnp.moveaxis(shard.reshape(*before, size, -1, *after), dim, 0)


def summed_on_arrival(shard, axis, dim):
    size = lax.axis_size(axis)
    parts = lax.all_to_all(cut_along(shard, dim, size), axis, 0, 0, tiled=True)
    return jnp.sum(parts, axis=0)


def total_of(shard, axes):
    lines = shard.reshape(-1, shard.shape[-1])
    padded = padded_to(lines, lax.axis_size(axes))
    whole = gathered_copies(summed_on_arrival(padded, axes, 0), axes, 0)
    return lax.slice_in_dim(whole, 0, len(lines)).reshape(shard.shape)


def conj_apply(factor, vector):
    parts = jnp.einsum("smk,tkn->stmn", factor, vector, precision=HIGHEST)
    return jnp.stack([parts[0, 0] + parts[1, 1], parts[0, 1] - parts[1, 0]])


def complex_apply(matrix, vector):
    parts = jnp.einsum("smk,tkn->stmn", matrix, vector, precision=HIGHEST)
    return jnp.stack([parts[0, 0] - parts[1, 1], parts[0, 1] + parts[1, 0]])


def column_reduce(terms):
    result = total_of(terms, "row")
    return result


def per_device(solved, upper_cols, coupling, inverse_diag, right_side):
    row_index = lax.axis_index("row")
    col_index = lax.axis_index("col")
    local_rows = inverse_diag.shape[2]
    local_cols = inverse_diag.shape[3]
    col_global = col_index * local_cols + jnp.arange(local_cols, dtype=jnp.int32)
    priors = jnp.einsum("spmk,tkn->stpmn", upper_cols, solved, precision=HIGHEST)
    prior_both = jnp.stack([priors[0, 0] + priors[1, 1], priors[0, 1] - priors[1, 0]])
    row_global = row_index * local_rows + jnp.arange(local_rows, dtype=jnp.int32)
    inverse = jnp.where(col_global[None, :] <= row_global[:, None], inverse_diag, 0.0)

    def finish(reduced, panel_index):
        partial_value = complex_apply(inverse[:, panel_index], reduced)
        result = total_of(partial_value, "col")
        return result

    total_first = column_reduce(prior_both[:, 0])
    answer_first = finish(right_side[:, 0] - total_first, 0)
    coupled = conj_apply(coupling, answer_first)
    reduced_second = right_side[:, 1] - column_reduce(prior_both[:, 1] + coupled)
    answer_second = finish(reduced_second, 1)
    return jnp.stack([answer_first, answer_second], axis=1)


def solution(mesh):
    in_specs = (
        P(None, "row", None),
        P(None, None, "col", "row"),
        P(None, "col", "row"),
        P(None, None, "row", "col"),
        P(None, None, "col", None),
    )
    out_specs = P(None, None, "row", None)
    return jax.shard_map(
        per_device, mesh=mesh, in_specs=in_specs, out_specs=out_specs, check_vma=False
    )
```

profile of v0, /device:TPU:1, one launch (start us, length us, event | category | flops | bytes accessed | tf_op | source)
XLA Modules:
  0.0 175.4 jit_solution(15890981241573187342)
XLA Ops:
  0.0 1.2 copy-done
  1.2 5.7 %fusion.2 = f32[2,2,2,64,512]{4,3,2,0,1:T(8,128)S(1)} fusion(f32[2,1024,512]{2,1,0:T(8,128)} %param.5, f32[2,2,64,1024]{3,2,1,0:T(8,128)S(1)} %copy-done), kind=kOutput, calls=%fused_computation.2 | convolution fusion | flops 3221225472 | bytes 6291456 | tf_op jit(solution)/shard_map/spmk,tkn->stpmn/dot_general | solution.py:73
  7.1 0.1 reshape_reshape_squeeze.3
  7.2 38.5 %all_to_all.40 = f32[32,4,512]{2,1,0:T(4,128)S(1)} all-to-all(f32[32,4,512]{2,1,0:T(4,128)S(1)} %reshape_reshape_squeeze.3), channel_id=1, replica_groups=mesh['row'=32,'col'=16] {'row'}, dimensions={0} | all-to-all | bytes 524288 | tf_op jit(solution)/shard_map/all_to_all | solution.py:41
  45.8 0.7 broadcast_in_dim.16
  46.6 4.5 %all-to-all-start.1 = ((f32[32,4,512]{2,1,0:T(4,128)}), f32[32,4,512]{2,1,0:T(4,128)S(1)}, u32[]{:S(2)}, u32[]{:S(2)}) async-start(f32[32,4,512]{2,1,0:T(4,128)} %broadcast_in_dim.16), calls=%async_computation.1 | async-start | bytes 524288 | tf_op jit(solution)/shard_map/all_to_all | solution.py:18
  51.2 21.9 %all-to-all-done.1 = f32[32,4,512]{2,1,0:T(4,128)S(1)} async-done(((f32[32,4,512]{2,1,0:T(4,128)}), f32[32,4,512]{2,1,0:T(4,128)S(1)}, u32[]{:S(2)}, u32[]{:S(2)}) %all-to-all-start.1) | async-done | bytes 262176 | tf_op jit(solution)/shard_map/all_to_all | solution.py:18
  73.1 0.1 reshape_reshape.16
  73.2 0.4 convolution_bitcast_fusion.2
  73.7 13.4 %all_to_all.41 = f32[16,4,512]{2,1,0:T(4,128)S(1)} all-to-all(f32[16,4,512]{2,1,0:T(4,128)S(1)} %reshape_reshape.17), channel_id=1, replica_groups=mesh['row'=32,'col'=16] {'col'}, dimensions={0} | all-to-all | bytes 262144 | tf_op jit(solution)/shard_map/all_to_all | solution.py:41
  87.2 0.7 broadcast_in_dim.19
  87.8 3.5 %all-to-all-start.3 = ((f32[16,4,512]{2,1,0:T(4,128)}), f32[16,4,512]{2,1,0:T(4,128)S(1)}, u32[]{:S(2)}, u32[]{:S(2)}) async-start(f32[16,4,512]{2,1,0:T(4,128)} %broadcast_in_dim.19), calls=%async_computation.3 | async-start | bytes 262144 | tf_op jit(solution)/shard_map/all_to_all | solution.py:18
  91.4 0.1 squeeze.7
  91.4 6.8 %all-to-all-done.3 = f32[16,4,512]{2,1,0:T(4,128)S(1)} async-done(((f32[16,4,512]{2,1,0:T(4,128)}), f32[16,4,512]{2,1,0:T(4,128)S(1)}, u32[]{:S(2)}, u32[]{:S(2)}) %all-to-all-start.3) | async-done | bytes 131104 | tf_op jit(solution)/shard_map/all_to_all | solution.py:18
  98.3 0.6 convolution_bitcast_fusion
  99.1 28.3 %all_to_all.42 = f32[32,4,512]{2,1,0:T(4,128)S(1)} all-to-all(f32[32,4,512]{2,1,0:T(4,128)S(1)} %add.86), channel_id=1, replica_groups=mesh['row'=32,'col'=16] {'row'}, dimensions={0} | all-to-all | bytes 524288 | tf_op jit(solution)/shard_map/all_to_all | solution.py:41
  127.5 25.8 %all_to_all.43 = f32[32,4,512]{2,1,0:T(4,128)S(1)} all-to-all(f32[32,4,512]{2,1,0:T(4,128)S(1)} %broadcast_in_dim.20), channel_id=1, replica_groups=mesh['row'=32,'col'=16] {'row'}, dimensions={0} | all-to-all | bytes 524288 | tf_op jit(solution)/shard_map/all_to_all | solution.py:18
  153.3 0.1 reshape_reshape.19
  153.4 0.4 convolution_bitcast_fusion.1
  153.9 9.7 %all_to_all.44 = f32[16,4,512]{2,1,0:T(4,128)S(1)} all-to-all(f32[16,4,512]{2,1,0:T(4,128)S(1)} %reshape_reshape.20), channel_id=1, replica_groups=mesh['row'=32,'col'=16] {'col'}, dimensions={0} | all-to-all | bytes 262144 | tf_op jit(solution)/shard_map/all_to_all | solution.py:41
  163.6 0.7 broadcast_in_dim.21
  164.3 3.5 %all-to-all-start.7 = ((f32[16,4,512]{2,1,0:T(4,128)}), f32[16,4,512]{2,1,0:T(4,128)S(1)}, u32[]{:S(2)}, u32[]{:S(2)}) async-start(f32[16,4,512]{2,1,0:T(4,128)} %broadcast_in_dim.21), calls=%async_computation.7 | async-start | bytes 262144 | tf_op jit(solution)/shard_map/all_to_all | solution.py:18
  167.9 6.8 %all-to-all-done.7 = f32[16,4,512]{2,1,0:T(4,128)S(1)} async-done(((f32[16,4,512]{2,1,0:T(4,128)}), f32[16,4,512]{2,1,0:T(4,128)S(1)}, u32[]{:S(2)}, u32[]{:S(2)}) %all-to-all-start.7) | async-done | bytes 131104 | tf_op jit(solution)/shard_map/all_to_all | solution.py:18
  174.7 0.7 pad_maximum_fusion.2
  (35 shorter events, 0.9 us)
Async XLA Ops:
  0.0 1.2 copy-start
  0.0 51.2 %copy-start.2 = (f32[2,2,32,64]{3,2,1,0:T(8,128)S(1)}, f32[2,2,32,64]{3,2,1,0:T(8,128)}, u32[]{:S(2)}) copy-start(f32[2,2,32,64]{3,2,1,0:T(8,128)} %param.8) | copy-start | bytes 98308
  7.0 66.2 %copy-start.1 = (f32[2,2,64,512]{3,2,1,0:T(8,128)S(1)}, f32[2,2,64,512]{3,2,1,0:T(8,128)}, u32[]{:S(2)}) copy-start(f32[2,2,64,512]{3,2,1,0:T(8,128)} %param.9) | copy-start | bytes 1572868
  7.0 91.3 %copy-start.3 = (f32[2,64,32]{1,2,0:T(8,128)S(1)}, f32[2,64,32]{1,2,0:T(8,128)}, u32[]{:S(2)}) copy-start(f32[2,64,32]{1,2,0:T(8,128)} %param.7) | copy-start | bytes 49156
  46.6 26.5 %all-to-all-start.1 = ((f32[32,4,512]{2,1,0:T(4,128)}), f32[32,4,512]{2,1,0:T(4,128)S(1)}, u32[]{:S(2)}, u32[]{:S(2)}) async-start(f32[32,4,512]{2,1,0:T(4,128)} %broadcast_in_dim.16), calls=%async_computation.1 | async-start | bytes 524288 | tf_op jit(solution)/shard_map/all_to_all | solution.py:18
  87.8 10.4 %all-to-all-start.3 = ((f32[16,4,512]{2,1,0:T(4,128)}), f32[16,4,512]{2,1,0:T(4,128)S(1)}, u32[]{:S(2)}, u32[]{:S(2)}) async-start(f32[16,4,512]{2,1,0:T(4,128)} %broadcast_in_dim.19), calls=%async_computation.3 | async-start | bytes 262144 | tf_op jit(solution)/shard_map/all_to_all | solution.py:18
  164.3 10.4 %all-to-all-start.7 = ((f32[16,4,512]{2,1,0:T(4,128)}), f32[16,4,512]{2,1,0:T(4,128)S(1)}, u32[]{:S(2)}, u32[]{:S(2)}) async-start(f32[16,4,512]{2,1,0:T(4,128)} %broadcast_in_dim.21), calls=%async_computation.7 | async-start | bytes 262144 | tf_op jit(solution)/shard_map/all_to_all | solution.py:18
where the time goes:
time: 177 us; the launch traced here: 175 us
  blocking collectives  116 us (66%)
  waiting for transfers between devices  35.5 us (20%)
  starting transfers between devices  11.5 us (6%)
  matrix products  7.1 us (4%)
  local copies, waits for them, and re-layouts  3.99 us (2%)
    all_to_all x4, blocking collectives, summed_on_arrival(): parts = lax.all_to_all(cut_along(shard, dim, size), axis, 0, 0, tiled=True)  89.9 us
    all_to_all x3, waiting for transfers between devices, sent_to_all(): lax.all_to_all(jnp.broadcast_to(shard[None], (size, *shard.shape)), axis,...  35.5 us
    all_to_all x1, blocking collectives, sent_to_all(): lax.all_to_all(jnp.broadcast_to(shard[None], (size, *shard.shape)), axis,...  25.8 us
    all_to_all x3, starting transfers between devices, sent_to_all(): lax.all_to_all(jnp.broadcast_to(shard[None], (size, *shard.shape)), axis,...  11.5 us
    dot_general x1, matrix products, per_device(): jnp.einsum('spmk,tkn->stpmn', upper_cols, solved, precision=HIGHEST)  5.73 us
  transfers between devices with their start and end apart: 3, of which 3 were waited for; matrix products, arithmetic and copies ran while one was open for 0% of the time, Pallas kernels for 0%

commit v1 on v0

v1 whole, which is shorter than its diff:
```python
import functools

import jax
import jax.numpy as jnp
from jax import lax
from jax.experimental import pallas as pl
from jax.experimental.pallas import tpu as pltpu
from jax.sharding import PartitionSpec as P

MESH = pl.DeviceIdType.MESH
F32 = jnp.float32
BF16 = jnp.bfloat16
NZ = 16
NC = 16
KSTEP = 256

Z_PRIOR, Z_CPL, Z_Q, Z_ANS = 0, 2, 3, 5
C_ANS, C_U, C_UALL, C_OUT = 0, 2, 3, 4
K_PRIOR, K_CPL, K_Q, K_ANS = 0, 2, 3, 5


def split(x):
    hi = x.astype(BF16)
    return hi, (x - hi.astype(F32)).astype(BF16)


def dot3(a, b):
    (ah, al), (bh, bl) = a, b
    dot = functools.partial(jnp.dot, preferred_element_type=F32)
    return dot(ah, bh) + (dot(ah, bl) + dot(al, bh))


def tile(i, size):
    return pl.ds(pl.multiple_of(i * size, size), size)


def far_first(t):
    half = (t + 1) // 2
    return 8 + jnp.where(lax.rem(t, 2) == 1, -half, half)


def kernel(
    s_hbm, u_hbm, rs_hbm, w_ref, ct_ref, o_ref,
    a_buf, s_buf, x_buf, pt, cx, p2, rb, rsb, rst, wh, wl, qa, cg, pu, ru, ug, ubh, ubl, pp, rc, ga, ob,
    load_sem, zs, zr, cs, cr, ks, kr,
):
    row = lax.axis_index("row")
    c = lax.axis_index("col")
    z, k = row // 2, lax.rem(row, 2)
    ok = 1 - k

    def z_dev(i):
        return (lax.rem(z + i, NZ) * 2 + k, c)

    def c_dev(i):
        return (row, lax.rem(c + i, NC))

    sibling = (z * 2 + ok, c)

    barrier = pltpu.get_barrier_semaphore()
    pl.semaphore_signal(barrier, inc=1, device_id=sibling, device_id_type=MESH)

    def greet(t, _):
        i = far_first(t)
        pl.semaphore_signal(barrier, inc=1, device_id=z_dev(i), device_id_type=MESH)
        pl.semaphore_signal(barrier, inc=1, device_id=c_dev(i), device_id_type=MESH)
        return 0

    lax.fori_loop(0, NZ - 1, greet, 0)

    def remote(src, dst, ssem, rsem, dev):
        return pltpu.make_async_remote_copy(
            src_ref=src, dst_ref=dst, send_sem=ssem, recv_sem=rsem, device_id=dev, device_id_type=MESH
        )

    def z_send(g, src, dst):
        def body(t, _):
            i = far_first(t)
            remote(src(lax.rem(z + i, NZ)), dst(z), zs.at[g, i], zr.at[g, i], z_dev(i)).start()
            return 0

        lax.fori_loop(0, NZ - 1, body, 0)

    def z_wait(g, i, src, dst):
        frm = lax.rem(z - i + NZ, NZ)
        remote(src(frm), dst(frm), zs.at[g, i], zr.at[g, i], z_dev(i)).wait_recv()
        return frm

    def z_wait_all(g, src, dst):
        def body(i, _):
            z_wait(g, i, src, dst)
            return 0

        lax.fori_loop(1, NZ, body, 0)

    def c_send(g, src, dst):
        def body(t, _):
            i = far_first(t)
            remote(src(lax.rem(c + i, NC)), dst(c), cs.at[g, i], cr.at[g, i], c_dev(i)).start()
            return 0

        lax.fori_loop(0, NC - 1, body, 0)

    def c_wait(g, i, src, dst):
        frm = lax.rem(c - i + NC, NC)
        remote(src(frm), dst(frm), cs.at[g, i], cr.at[g, i], c_dev(i)).wait_recv()
        return frm

    def c_wait_all(g, src, dst):
        def body(i, _):
            c_wait(g, i, src, dst)
            return 0

        lax.fori_loop(1, NC, body, 0)

    def k_copy(g, src, dst):
        return remote(src, dst, ks.at[g], kr.at[g], sibling)

    loads_a = [
        pltpu.make_async_copy(u_hbm.at[s, p], a_buf.at[pl.ds((p * 2 + s) * 64, 64)], load_sem.at[p * 2 + s])
        for p in range(2)
        for s in range(2)
    ]

    def load_s(s, j):
        return pltpu.make_async_copy(
            s_hbm.at[s, tile(j, KSTEP)], s_buf.at[s, tile(j, KSTEP)], load_sem.at[8 + s * 4 + j]
        )

    block = k * 2 + z // 8
    loads_r = [
        pltpu.make_async_copy(
            rs_hbm.at[s, p, :, tile(block, 128)], rsb.at[p, pl.ds(s * 64, 64)], load_sem.at[4 + p * 2 + s]
        )
        for p in range(2)
        for s in range(2)
    ]
    for copy in loads_a:
        copy.start()
    for j in range(4):
        load_s(0, j).start()
        load_s(1, j).start()
    for copy in loads_r:
        copy.start()

    for copy in loads_a:
        copy.wait()

    def prior_step(j, _):
        a = split(a_buf[:, tile(j, KSTEP)])
        for s in range(2):
            load_s(s, j).wait()
            part = dot3(a, split(s_buf[s, tile(j, KSTEP), :]))

            @pl.when(j == 0)
            def _():
                x_buf[s] = part

            @pl.when(j > 0)
            def _():
                x_buf[s] += part

        return 0

    lax.fori_loop(0, 4, prior_step, 0)
    for p in range(2):
        lo, mid, hi = p * 128, p * 128 + 64, p * 128 + 128
        re = x_buf[0, lo:mid] + x_buf[1, mid:hi]
        im = x_buf[1, lo:mid] - x_buf[0, mid:hi]
        pt[p] = jnp.concatenate([re, im], axis=0).T
    for copy in loads_r:
        copy.wait()
    for p in range(2):
        rst[p] = rsb[p].T
        wh[p], wl[p] = split(w_ref[p])
    own_ct = cg.at[tile(z, 32), tile(k, 128)]
    own_ct[...] = ct_ref[...]

    pl.semaphore_wait(barrier, 1 + (NZ - 1) + (NC - 1))

    for p in range(2):
        k_copy(K_PRIOR + p, pt.at[p, tile(ok, 256)], cx.at[p]).start()
    for p in range(2):
        k_copy(K_PRIOR + p, pt.at[p, tile(ok, 256)], cx.at[p]).wait_recv()
        p2[p] = pt[p, tile(k, 256)] + cx[p]
        z_send(Z_PRIOR + p, lambda i: p2.at[p, tile(i, 16)], lambda i: rb.at[p, tile(i, 16)])
    z_send(Z_CPL, lambda i: own_ct, lambda i: cg.at[tile(i, 32), tile(k, 128)])

    for p in range(2):

        def arrived(i, total):
            frm = z_wait(Z_PRIOR + p, i, lambda i: p2.at[p, tile(i, 16)], lambda i: rb.at[p, tile(i, 16)])
            return total + rb[p, tile(frm, 16)]

        total = lax.fori_loop(1, NZ, arrived, p2[p, tile(z, 16)])
        own_q = qa.at[p, tile(z, 16), tile(k, 128)]
        own_q[...] = rst[p, tile(lax.rem(z, 8), 16)] - total
        z_send(Z_Q + p, lambda i: own_q, lambda i: qa.at[p, tile(i, 16), tile(k, 128)])

    z_wait_all(Z_CPL, lambda i: own_ct, lambda i: cg.at[tile(i, 32), tile(k, 128)])
    half = cg.at[:, tile(k, 128)]
    k_copy(K_CPL, half, half).start()
    k_copy(K_CPL, half, cg.at[:, tile(ok, 128)]).wait_recv()
    pu[...] = dot3(split(cg[...]), (wh[1], wl[1]))
    c_send(C_U, lambda i: pu.at[tile(i, 32)], lambda i: ru.at[tile(i, 32)])

    def lower(p):
        z_wait_all(Z_Q + p, lambda i: qa.at[p, tile(z, 16), tile(k, 128)], lambda i: qa.at[p, tile(i, 16), tile(k, 128)])
        half = qa.at[p, :, tile(k, 128)]
        k_copy(K_Q + p, half, half).start()
        k_copy(K_Q + p, half, qa.at[p, :, tile(ok, 128)]).wait_recv()
        pp[p] = dot3(split(qa[p]), (wh[p], wl[p]))
        c_send(C_ANS + p, lambda i: pp.at[p, tile(i, 16)], lambda i: rc.at[p, tile(i, 16)])

    def summed(p):
        def arrived(i, total):
            frm = c_wait(C_ANS + p, i, lambda i: pp.at[p, tile(i, 16)], lambda i: rc.at[p, tile(i, 16)])
            return total + rc[p, tile(frm, 16)]

        return lax.fori_loop(1, NC, arrived, pp[p, tile(c, 16)])

    def share(p, answer):
        own = ob.at[p, tile(c, 16)]
        own[...] = answer
        c_send(C_OUT + p, lambda i: own, lambda i: ob.at[p, tile(i, 16)])

    lower(0)

    def u_arrived(i, total):
        frm = c_wait(C_U, i, lambda i: pu.at[tile(i, 32)], lambda i: ru.at[tile(i, 32)])
        return total + ru[tile(frm, 32)]

    own_u = ug.at[tile(c, 32)]
    own_u[...] = lax.fori_loop(1, NC, u_arrived, pu[tile(c, 32)])
    c_send(C_UALL, lambda i: own_u, lambda i: ug.at[tile(i, 32)])

    answer_0 = summed(0)
    slot = k * NZ
    own_a = ga.at[:, tile(slot + z, 128)]
    own_a[...] = answer_0
    z_send(Z_ANS, lambda i: own_a, lambda i: ga.at[:, tile(slot + i, 128)])
    share(0, answer_0)

    lower(1)

    c_wait_all(C_UALL, lambda i: own_u, lambda i: ug.at[tile(i, 32)])
    lane = lax.broadcasted_iota(jnp.int32, (32, 128), 1)
    left = lane < 64
    imag = lax.rem(lane // 32, 2) == 1

    def weigh(i, _):
        v = ug[tile(i, 32)]
        v2 = jnp.where(imag, pltpu.roll(v, 32, 1), -pltpu.roll(v, 96, 1))
        t, t2 = pltpu.roll(v, 64, 1), pltpu.roll(v2, 64, 1)
        zero = jnp.zeros_like(v)
        for par, parts in enumerate([(v, v2, t, t2), (t, t2, v, v2)]):
            rows = jnp.concatenate(
                [
                    jnp.where(left, parts[0], zero),
                    jnp.where(left, parts[1], zero),
                    jnp.where(left, zero, parts[2]),
                    jnp.where(left, zero, parts[3]),
                ],
                axis=0,
            )
            hi, lo = split(rows)
            ubh[tile(par * NZ + i, 128)] = hi
            ubl[tile(par * NZ + i, 128)] = lo
        return 0

    lax.fori_loop(0, NC, weigh, 0)
    own_1 = summed(1)

    z_wait_all(Z_ANS, lambda i: own_a, lambda i: ga.at[:, tile(slot + i, 128)])
    half_a = ga.at[:, tile(k, NZ * 128)]
    k_copy(K_ANS, half_a, half_a).start()
    k_copy(K_ANS, half_a, ga.at[:, tile(ok, NZ * 128)]).wait_recv()
    share(1, own_1 - dot3(split(ga[...]), (ubh[...], ubl[...])))

    for p in range(2):
        c_wait_all(C_OUT + p, lambda i: ob.at[p, tile(c, 16)], lambda i: ob.at[p, tile(i, 16)])
        turned = ob[p].T
        for h in range(2):
            for s in range(2):
                at = (h * 2 + s) * 32
                o_ref[s, p, :, pl.ds(h * 256, 256)] = turned[at : at + 32]

    def drain(i, _):
        blk, big, act = rb.at[0, pl.ds(0, 16)], ru.at[pl.ds(0, 32)], ga.at[:, pl.ds(0, 128)]
        q = qa.at[0, pl.ds(0, 16), pl.ds(0, 128)]
        ctb = cg.at[pl.ds(0, 32), pl.ds(0, 128)]
        for g, ref in ((0, blk), (1, blk), (2, ctb), (3, q), (4, q), (5, act)):
            remote(ref, ref, zs.at[g, i], zr.at[g, i], z_dev(i)).wait_send()
        for g, ref in ((0, blk), (1, blk), (2, big), (3, big), (4, blk), (5, blk)):
            remote(ref, ref, cs.at[g, i], cr.at[g, i], c_dev(i)).wait_send()
        return 0

    lax.fori_loop(1, NZ, drain, 0)
    k_copy(0, cx.at[0], cx.at[0]).wait_send()
    k_copy(1, cx.at[1], cx.at[1]).wait_send()
    k_copy(2, half, half).wait_send()
    for p in range(2):
        hq = qa.at[p, :, tile(k, 128)]
        k_copy(K_Q + p, hq, hq).wait_send()
    k_copy(K_ANS, half_a, half_a).wait_send()


def per_device(solved, upper_cols, coupling, inverse_diag, right_side):
    rows, cols = inverse_diag.shape[2], inverse_diag.shape[3]
    row_global = lax.axis_index("row") * rows + jnp.arange(rows, dtype=jnp.int32)
    col_global = lax.axis_index("col") * cols + jnp.arange(cols, dtype=jnp.int32)
    low = jnp.where(col_global[None, :] <= row_global[:, None], inverse_diag, 0.0)
    re, im = jnp.swapaxes(low[0], 1, 2), jnp.swapaxes(low[1], 1, 2)
    w = jnp.concatenate([jnp.concatenate([re, im], 2), jnp.concatenate([-im, re], 2)], 1)
    none = jnp.zeros_like(w)
    w = jnp.concatenate([jnp.concatenate([w, none], 2), jnp.concatenate([none, w], 2)], 1)
    ct = jnp.concatenate([coupling[0].T, -coupling[1].T], 1)
    vmem = pl.BlockSpec(memory_space=pltpu.VMEM)
    hbm = pl.BlockSpec(memory_space=pltpu.HBM)
    f = lambda *shape: pltpu.VMEM(shape, F32)
    b = lambda *shape: pltpu.VMEM(shape, BF16)
    return pl.pallas_call(
        kernel,
        out_shape=jax.ShapeDtypeStruct((2, 2, 32, 512), F32),
        in_specs=[hbm, hbm, hbm, vmem, vmem],
        out_specs=vmem,
        scratch_shapes=[
            f(256, 1024), f(2, 1024, 512), f(2, 256, 512), f(2, 512, 128), f(2, 256, 128), f(2, 256, 128),
            f(2, 256, 128), f(2, 128, 128), f(2, 128, 128), b(2, 256, 128), b(2, 256, 128), f(2, 256, 256),
            f(512, 256), f(512, 128), f(512, 128), f(512, 128), b(4096, 128), b(4096, 128), f(2, 256, 128),
            f(2, 256, 128), f(16, 4096), f(2, 256, 128),
            pltpu.SemaphoreType.DMA((16,)),
            pltpu.SemaphoreType.DMA((6, 16)), pltpu.SemaphoreType.DMA((6, 16)),
            pltpu.SemaphoreType.DMA((6, 16)), pltpu.SemaphoreType.DMA((6, 16)),
            pltpu.SemaphoreType.DMA((6,)), pltpu.SemaphoreType.DMA((6,)),
        ],
        compiler_params=pltpu.CompilerParams(
            collective_id=0, has_side_effects=True, vmem_limit_bytes=48 * 1024 * 1024
        ),
        name="panels",
    )(solved, upper_cols, right_side, w, ct)


def solution(mesh):
    in_specs = (
        P(None, "row", None),
        P(None, None, "col", "row"),
        P(None, "col", "row"),
        P(None, None, "row", "col"),
        P(None, None, "col", None),
    )
    out_specs = P(None, None, "row", None)
    return jax.shard_map(
        per_device, mesh=mesh, in_specs=in_specs, out_specs=out_specs, check_vma=False
    )
```

time: 177 us -> 81.1 us (0.46)
  blocking collectives: 116 us -> 0 us
  Pallas kernels: 0 us -> 75.7 us
  waiting for transfers between devices: 35.5 us -> 0 us
  starting transfers between devices: 11.5 us -> 0 us
  matrix products: 7.1 us -> 0 us
    all_to_all x5 -> x0, blocking collectives: 116 us -> none  [the longest x4 89.9 us: summed_on_arrival(): parts = lax.all_to_all(cut_along(shard, dim, size), axis, 0, 0, tiled=True)]
    pallas_call x0 -> x1, Pallas kernels: none -> 75.7 us  [per_device(): pl.pallas_call(kernel, out_shape=jax.ShapeDtypeStruct((2, 2, 32, 512), F3...]
    all_to_all x3 -> x0, waiting for transfers between devices: 35.5 us -> none  [sent_to_all(): lax.all_to_all(jnp.broadcast_to(shard[None], (size, *shard.shape)), axis,...]
    all_to_all x3 -> x0, starting transfers between devices: 11.5 us -> none  [sent_to_all(): lax.all_to_all(jnp.broadcast_to(shard[None], (size, *shard.shape)), axis,...]
    dot_general x4 -> x0, matrix products: 7.1 us -> none  [the longest x1 5.73 us: per_device(): jnp.einsum('spmk,tkn->stpmn', upper_cols, solved, precision=HIGHEST)]
    unnamed x8 -> x6, local copies, waits for them, and re-layouts: 1.24 us -> 3.9 us
    broadcast_in_dim x4 -> x0, local copies, waits for them, and re-layouts: 2.13 us -> none  [sent_to_all(): jnp.broadcast_to(shard[None], (size, *shard.shape))]
  transfers between devices with their start and end apart: 3 -> 0, of which waited for: 3 -> 0; matrix products, arithmetic and copies ran while one was open for 0% -> 0% of each run, Pallas kernels for 0% -> 0%
where the time goes in v1:
time: 81.1 us; the launch traced here: 80.8 us
  Pallas kernels  75.7 us (93%)
  local copies, waits for them, and re-layouts  3.91 us (5%)
  other arithmetic  1.12 us (1%)
    pallas_call x1, Pallas kernels, per_device(): pl.pallas_call(kernel, out_shape=jax.ShapeDtypeStruct((2, 2, 32, 512), F3...  75.7 us
    unnamed x6, local copies, waits for them, and re-layouts  3.9 us

profile of v1, /device:TPU:1, one launch (start us, length us, event | category | flops | bytes accessed | tf_op | source)
XLA Modules:
  0.0 80.8 jit_solution(12614079810980303071)
XLA Ops:
  0.0 0.1 broadcast_compare_fusion
  0.1 0.7 slice_bitcast_fusion.2
  0.8 0.1 pad_maximum_fusion.ct_ref
  0.9 0.9 %copy.6 = f32[2,2,32,64]{2,3,1,0:T(8,128)S(1)} copy(f32[2,2,32,64]{3,2,1,0:T(8,128)} %param.8) | data formatting | bytes 65536 | tf_op args[3]
  1.9 0.1 maximum_maximum_fusion
  2.0 0.1 select_maximum_fusion.w_ref
  2.1 0.0 copy-start
  2.1 1.2 %copy-done = f32[2,2,64,1024]{3,2,1,0:T(8,128)S(1)} copy-done((f32[2,2,64,1024]{3,2,1,0:T(8,128)S(1)}, f32[2,2,64,1024]{3,2,1,0:T(8,128)}, u32[]{:S(2)}) %copy-start) | copy-done | bytes 1048600
  3.3 0.0 copy-start.1
  3.3 1.0 %copy-done.1 = f32[2,2,64,512]{3,2,1,0:T(8,128)S(1)} copy-done((f32[2,2,64,512]{3,2,1,0:T(8,128)S(1)}, f32[2,2,64,512]{3,2,1,0:T(8,128)}, u32[]{:S(2)}) %copy-start.1) | copy-done | bytes 524312
  4.4 75.7 %panels.1 = f32[2,2,32,512]{3,2,1,0:T(8,128)S(1)} custom-call(f32[2,1024,512]{2,1,0:T(8,128)} %s_hbm.1, f32[2,2,64,1024]{3,2,1,0:T(8,128)S(1)} %copy-done, f32[2,2,64,512]{3,2,1,0:T(8,128)S(1)} %copy-done.1, f32[2,256,128]{2,1,0:T(8,128)S(1)} %select_maximum_fusion.w_ref, f32[32,128]{1,0:T(8,128)S(1)} %pad_maximum_fusion.ct_ref), custom_call_target="tpu_custom_call" | custom-call | tf_op jit(solution)/shard_map/panels/pallas_call | solution.py:322
  80.1 0.7 copy.8
  (5 shorter events, 0.0 us)
Async XLA Ops:
  2.1 1.2 %copy-start = (f32[2,2,64,1024]{3,2,1,0:T(8,128)S(1)}, f32[2,2,64,1024]{3,2,1,0:T(8,128)}, u32[]{:S(2)}) copy-start(f32[2,2,64,1024]{3,2,1,0:T(8,128)} %u_hbm.1) | copy-start | bytes 3145732
  3.3 1.0 %copy-start.1 = (f32[2,2,64,512]{3,2,1,0:T(8,128)S(1)}, f32[2,2,64,512]{3,2,1,0:T(8,128)}, u32[]{:S(2)}) copy-start(f32[2,2,64,512]{3,2,1,0:T(8,128)} %rs_hbm.1) | copy-start | bytes 1572868

commit v2 on v1

v2 whole, which is shorter than its diff:
```python
import functools

import jax
import jax.numpy as jnp
from jax import lax
from jax.experimental import pallas as pl
from jax.experimental.pallas import tpu as pltpu
from jax.sharding import PartitionSpec as P

MESH = pl.DeviceIdType.MESH
F32 = jnp.float32
BF16 = jnp.bfloat16
NZ = 16
NC = 16
KSTEP = 512
VMEM = 62 * 1024 * 1024

Z_PRIOR, Z_CPL, Z_Q, Z_ANS, Z_CPL2 = 0, 2, 3, 5, 6
C_ANS, C_U, C_UALL, C_OUT = 0, 2, 3, 4
K_PRIOR, K_INV, K_OUT, K_U = 0, 2, 3, 5


def split(x):
    hi = x.astype(BF16)
    return hi, (x - hi.astype(F32)).astype(BF16)


def dot3(a, b):
    (ah, al), (bh, bl) = a, b
    dot = functools.partial(jnp.dot, preferred_element_type=F32)
    return dot(ah, bh) + (dot(ah, bl) + dot(al, bh))


def tile(i, size):
    return pl.ds(i * size if isinstance(i, int) else pl.multiple_of(i * size, size), size)


def far_first(t):
    half = (t + 1) // 2
    return 8 + jnp.where(lax.rem(t, 2) == 1, -half, half)


def place(z):
    return lax.rem(z, 4) * 4 + z // 4


def kernel(
    s_hbm, u_hbm, rs_hbm, d_hbm, c_hbm, o_ref,
    d_buf, c_buf, a_buf, s_buf, x_buf, pt, cx, p2, rb, rsb, rst, wh, wl, qa, cg, pu, ru, ug, ubh, ubl, pp, rc, ga, xb, xs, ob,
    load_sem, zs, zr, cs, cr, ks, kr,
):
    row = lax.axis_index("row")
    c = lax.axis_index("col")
    z, k = row // 2, lax.rem(row, 2)
    ok = 1 - k

    def z_dev(i):
        return (lax.rem(z + i, NZ) * 2 + k, c)

    def c_dev(i):
        return (row, lax.rem(c + i, NC))

    sibling = (z * 2 + ok, c)

    barrier = pltpu.get_barrier_semaphore()
    pl.semaphore_signal(barrier, inc=1, device_id=sibling, device_id_type=MESH)

    def greet(t, _):
        i = far_first(t)
        pl.semaphore_signal(barrier, inc=1, device_id=z_dev(i), device_id_type=MESH)
        pl.semaphore_signal(barrier, inc=1, device_id=c_dev(i), device_id_type=MESH)
        return 0

    lax.fori_loop(0, NZ - 1, greet, 0)

    def remote(src, dst, ssem, rsem, dev):
        return pltpu.make_async_remote_copy(
            src_ref=src, dst_ref=dst, send_sem=ssem, recv_sem=rsem, device_id=dev, device_id_type=MESH
        )

    def z_send(g, src, dst):
        def body(t, _):
            i = far_first(t)
            remote(src(lax.rem(z + i, NZ)), dst(z), zs.at[g, i], zr.at[g, i], z_dev(i)).start()
            return 0

        lax.fori_loop(0, NZ - 1, body, 0)

    def z_wait(g, i, src, dst):
        frm = lax.rem(z - i + NZ, NZ)
        remote(src(frm), dst(frm), zs.at[g, i], zr.at[g, i], z_dev(i)).wait_recv()
        return frm

    def z_wait_all(g, src, dst):
        def body(i, _):
            z_wait(g, i, src, dst)
            return 0

        lax.fori_loop(1, NZ, body, 0)

    def c_send(g, src, dst):
        def body(t, _):
            i = far_first(t)
            remote(src(lax.rem(c + i, NC)), dst(c), cs.at[g, i], cr.at[g, i], c_dev(i)).start()
            return 0

        lax.fori_loop(0, NC - 1, body, 0)

    def c_wait(g, i, src, dst):
        frm = lax.rem(c - i + NC, NC)
        remote(src(frm), dst(frm), cs.at[g, i], cr.at[g, i], c_dev(i)).wait_recv()
        return frm

    def c_wait_all(g, src, dst):
        def body(i, _):
            c_wait(g, i, src, dst)
            return 0

        lax.fori_loop(1, NC, body, 0)

    def k_copy(g, src, dst):
        return remote(src, dst, ks.at[g], kr.at[g], sibling)

    loads_a = [
        pltpu.make_async_copy(u_hbm.at[s, p], a_buf.at[pl.ds((p * 2 + s) * 64, 64)], load_sem.at[p * 2 + s])
        for p in range(2)
        for s in range(2)
    ]

    def load_s(s, j):
        return pltpu.make_async_copy(
            s_hbm.at[s, tile(j, KSTEP)], s_buf.at[s, tile(j, KSTEP)], load_sem.at[8 + s * 4 + j]
        )

    block = k * 2 + z // 8
    loads_r = [
        pltpu.make_async_copy(
            rs_hbm.at[s, p, :, tile(block, 128)], rsb.at[p, pl.ds(s * 64, 64)], load_sem.at[4 + p * 2 + s]
        )
        for p in range(2)
        for s in range(2)
    ]
    loads_r.append(pltpu.make_async_copy(d_hbm, d_buf.at[k], load_sem.at[16]))
    loads_r.append(pltpu.make_async_copy(c_hbm, c_buf, load_sem.at[17]))
    for copy in loads_a:
        copy.start()
    for j in range(1024 // KSTEP):
        load_s(0, j).start()
        load_s(1, j).start()
    for copy in loads_r:
        copy.start()

    for copy in loads_a:
        copy.wait()

    def prior_step(j, _):
        a = split(a_buf[:, tile(j, KSTEP)])
        for s in range(2):
            load_s(s, j).wait()
            part = dot3(a, split(s_buf[s, tile(j, KSTEP), :]))

            if j == 0:
                x_buf[s] = part
            else:
                x_buf[s] += part

    for j in range(1024 // KSTEP):
        prior_step(j, 0)
    for copy in loads_r:
        copy.wait()
    own_ct = cg.at[tile(place(z), 32)]
    own_ct[...] = jnp.concatenate([c_buf[0], -c_buf[1]], 1)

    pl.semaphore_wait(barrier, 1 + (NZ - 1) + (NC - 1))

    def cpl_copy(i):
        return remote(own_ct, own_ct, zs.at[Z_CPL, i], zr.at[Z_CPL, i], z_dev(i))

    for i in (8, 4, 12):
        cpl_copy(i).start()
    own_d = d_buf.at[k]
    k_copy(K_INV, own_d, own_d).start()

    for p in range(2):
        lo, mid, hi = p * 128, p * 128 + 64, p * 128 + 128
        re = x_buf[0, lo:mid] + x_buf[1, mid:hi]
        im = x_buf[1, lo:mid] - x_buf[0, mid:hi]
        pt[p] = jnp.concatenate([re, im], axis=0).T
        k_copy(K_PRIOR + p, pt.at[p, tile(ok, 256)], cx.at[p]).start()
    for p in range(2):
        k_copy(K_PRIOR + p, pt.at[p, tile(ok, 256)], cx.at[p]).wait_recv()
        p2[p] = pt[p, tile(k, 256)] + cx[p]
        z_send(Z_PRIOR + p, lambda i: p2.at[p, tile(i, 16)], lambda i: rb.at[p, tile(i, 16)])
    for p in range(2):
        rst[p] = rsb[p].T
    k_copy(K_INV, own_d, d_buf.at[ok]).wait_recv()
    at = lax.broadcasted_iota(jnp.int32, (32, 64), 0) - lax.broadcasted_iota(jnp.int32, (32, 64), 1)
    for p in range(2):
        lines = []
        for q in range(2):
            low = c * 64 <= at + (z * 64 + q * 32)
            re, im = (jnp.where(low, d_buf[q, s, p], 0.0) for s in range(2))
            lines += [jnp.concatenate([re, -im], 1), jnp.concatenate([im, re], 1)]
        wh[p], wl[p] = split(jnp.concatenate(lines, 0).T)

    onward = ((0, 1, 0, 128), (1, -1, 0, 128), (2, 2, 0, 64), (3, -2, 64, 64))

    def onward_copy(n, step, first, rows, frm):
        ref = cg.at[pl.ds(pl.multiple_of(lax.rem(frm, 4) * 128 + first, 64), rows)]
        return remote(ref, ref, zs.at[Z_CPL2, n], zr.at[Z_CPL2, n], z_dev(step + NZ))

    for i in (4, 8, 12):
        cpl_copy(i).wait_recv()
    for n, step, first, rows in onward:
        onward_copy(n, step, first, rows, z).start()

    def gather_q(p):
        def arrived(i, total):
            frm = z_wait(Z_PRIOR + p, i, lambda i: p2.at[p, tile(i, 16)], lambda i: rb.at[p, tile(i, 16)])
            return total + rb[p, tile(frm, 16)]

        total = lax.fori_loop(1, NZ, arrived, p2[p, tile(z, 16)])
        own_q = qa.at[p, tile(z, 16)]
        own_q[...] = rst[p, tile(lax.rem(z, 8), 16)] - total
        z_send(Z_Q + p, lambda i: own_q, lambda i: qa.at[p, tile(i, 16)])

    gather_q(0)

    for n, step, first, rows in onward:
        onward_copy(n, step, first, rows, z - step + NZ).wait_recv()
    pu[...] = dot3(split(cg[...]), (wh[1], wl[1]))
    c_send(C_U, lambda i: pu.at[tile(i, 32)], lambda i: ru.at[tile(i, 32)])
    gather_q(1)

    def lower(p):
        z_wait_all(Z_Q + p, lambda i: qa.at[p, tile(z, 16)], lambda i: qa.at[p, tile(i, 16)])
        pp[p] = dot3(split(qa[p]), (wh[p], wl[p]))
        c_send(C_ANS + p, lambda i: pp.at[p, tile(i, 16)], lambda i: rc.at[p, tile(i, 16)])

    def summed(p):
        def arrived(i, total):
            frm = c_wait(C_ANS + p, i, lambda i: pp.at[p, tile(i, 16)], lambda i: rc.at[p, tile(i, 16)])
            return total + rc[p, tile(frm, 16)]

        return lax.fori_loop(1, NC, arrived, pp[p, tile(c, 16)])

    lane = lax.broadcasted_iota(jnp.int32, (16, 128), 1)
    own_lanes = lane // 64 == k

    def swap(p):
        return k_copy(K_OUT + p, xb.at[p], xs.at[p])

    def share(p):
        swap(p).wait_recv()
        own = ob.at[p, tile(c, 16)]
        own[...] = jnp.where(own_lanes, xb[p], pltpu.roll(xs[p], 64, 1))
        c_send(C_OUT + p, lambda i: own, lambda i: ob.at[p, tile(i, 16)])

    lower(0)

    def u_arrived(i, total):
        frm = c_wait(C_U, i, lambda i: pu.at[tile(i, 32)], lambda i: ru.at[tile(i, 32)])
        return total + ru[tile(frm, 32)]

    own_u = ug.at[k, tile(c, 32)]
    own_u[...] = lax.fori_loop(1, NC, u_arrived, pu[tile(c, 32)])
    c_send(C_UALL, lambda i: own_u, lambda i: ug.at[k, tile(i, 32)])

    own_a = ga.at[:, tile(z, 128)]
    answer_0 = summed(0)
    own_a[...] = answer_0
    z_send(Z_ANS, lambda i: own_a, lambda i: ga.at[:, tile(i, 128)])
    xb[0] = answer_0
    swap(0).start()

    lower(1)

    c_wait_all(C_UALL, lambda i: own_u, lambda i: ug.at[k, tile(i, 32)])
    half = ug.at[k]
    k_copy(K_U, half, half).start()
    share(0)

    k_copy(K_U, half, ug.at[ok]).wait_recv()
    imag = lax.rem(lax.broadcasted_iota(jnp.int32, (32, 128), 1) // 32, 2) == 1

    def weigh(i, _):
        for q in range(2):
            v = ug[q, tile(i, 32)]
            v2 = jnp.where(imag, pltpu.roll(v, 32, 1), -pltpu.roll(v, 96, 1))
            hi, lo = split(jnp.concatenate([v, v2], axis=0))
            ubh[tile(place(i) * 2 + q, 64)] = hi
            ubl[tile(place(i) * 2 + q, 64)] = lo
        return 0

    lax.fori_loop(0, NC, weigh, 0)
    own_1 = summed(1)

    z_wait_all(Z_ANS, lambda i: own_a, lambda i: ga.at[:, tile(i, 128)])
    xb[1] = own_1 - dot3(split(ga[...]), (ubh[...], ubl[...]))
    swap(1).start()
    share(1)

    for p in range(2):
        c_wait_all(C_OUT + p, lambda i: ob.at[p, tile(c, 16)], lambda i: ob.at[p, tile(i, 16)])
        turned = ob[p].T
        for h in range(2):
            for s in range(2):
                at = (h * 2 + s) * 32
                o_ref[s, p, :, pl.ds(h * 256, 256)] = turned[at : at + 32]

    def drain(i, _):
        blk, big, act = rb.at[0, pl.ds(0, 16)], ru.at[pl.ds(0, 32)], ga.at[:, pl.ds(0, 128)]
        q = qa.at[0, pl.ds(0, 16)]
        for g, ref in ((0, blk), (1, blk), (3, q), (4, q), (5, act)):
            remote(ref, ref, zs.at[g, i], zr.at[g, i], z_dev(i)).wait_send()
        for g, ref in ((0, blk), (1, blk), (2, big), (3, big), (4, blk), (5, blk)):
            remote(ref, ref, cs.at[g, i], cr.at[g, i], c_dev(i)).wait_send()
        return 0

    lax.fori_loop(1, NZ, drain, 0)
    for i in (4, 8, 12):
        cpl_copy(i).wait_send()
    for n, step, first, rows in onward:
        onward_copy(n, step, first, rows, z).wait_send()
    k_copy(0, cx.at[0], cx.at[0]).wait_send()
    k_copy(1, cx.at[1], cx.at[1]).wait_send()
    k_copy(K_INV, own_d, own_d).wait_send()
    k_copy(K_U, half, half).wait_send()
    for p in range(2):
        swap(p).wait_send()


def per_device(solved, upper_cols, coupling, inverse_diag, right_side):
    vmem = pl.BlockSpec(memory_space=pltpu.VMEM)
    hbm = pl.BlockSpec(memory_space=pltpu.HBM)
    f = lambda *shape: pltpu.VMEM(shape, F32)
    b = lambda *shape: pltpu.VMEM(shape, BF16)
    return pl.pallas_call(
        kernel,
        out_shape=pltpu.VMEM((2, 2, 32, 512), F32),
        in_specs=[hbm] * 5,
        out_specs=vmem,
        scratch_shapes=[
            f(2, 2, 2, 32, 64), f(2, 32, 64), f(256, 1024), f(2, 1024, 512), f(2, 256, 512), f(2, 512, 128),
            f(2, 256, 128), f(2, 256, 128), f(2, 256, 128), f(2, 128, 128), f(2, 128, 128),
            b(2, 128, 128), b(2, 128, 128), f(2, 256, 128), f(512, 128), f(512, 128), f(512, 128), f(2, 512, 128),
            b(2048, 128), b(2048, 128), f(2, 256, 128), f(2, 256, 128), f(16, 2048), f(2, 16, 128), f(2, 16, 128),
            f(2, 256, 128),
            pltpu.SemaphoreType.DMA((18,)),
            pltpu.SemaphoreType.DMA((7, 16)), pltpu.SemaphoreType.DMA((7, 16)),
            pltpu.SemaphoreType.DMA((6, 16)), pltpu.SemaphoreType.DMA((6, 16)),
            pltpu.SemaphoreType.DMA((6,)), pltpu.SemaphoreType.DMA((6,)),
        ],
        compiler_params=pltpu.CompilerParams(
            collective_id=0, has_side_effects=True, vmem_limit_bytes=VMEM
        ),
        name="panels",
    )(solved, upper_cols, right_side, inverse_diag, jnp.swapaxes(coupling, 1, 2))


def solution(mesh):
    in_specs = (
        P(None, "row", None),
        P(None, None, "col", "row"),
        P(None, "col", "row"),
        P(None, None, "row", "col"),
        P(None, None, "col", None),
    )
    out_specs = P(None, None, "row", None)
    return jax.shard_map(
        per_device, mesh=mesh, in_specs=in_specs, out_specs=out_specs, check_vma=False
    )
```

time: 81.1 us -> 67.5 us (0.83)
  Pallas kernels: 75.7 us -> 66.6 us
  local copies, waits for them, and re-layouts: 3.91 us -> 0.71 us
  other arithmetic: 1.12 us -> 0 us
    pallas_call x1, Pallas kernels: 75.7 us -> 66.6 us  [per_device(): pl.pallas_call(kernel, out_shape=pltpu.VMEM((2, 2, 32, 512), F32), in_spe...]
    unnamed x6 -> x1, local copies, waits for them, and re-layouts: 3.9 us -> 0.71 us
where the time goes in v2:
time: 67.5 us; the launch traced here: 67.3 us
  Pallas kernels  66.6 us (99%)
  local copies, waits for them, and re-layouts  0.71 us (1%)
    pallas_call x1, Pallas kernels, per_device(): pl.pallas_call(kernel, out_shape=pltpu.VMEM((2, 2, 32, 512), F32), in_spe...  66.6 us

profile of v2, /device:TPU:1, one launch (start us, length us, event | category | flops | bytes accessed | tf_op | source)
XLA Modules:
  0.0 67.3 jit_solution(4036177661676542573)
XLA Ops:
  0.0 66.6 %panels.1 = f32[2,2,32,512]{3,2,1,0:T(8,128)S(1)} custom-call(f32[2,1024,512]{2,1,0:T(8,128)} %s_hbm.1, f32[2,2,64,1024]{3,2,1,0:T(8,128)} %u_hbm.1, f32[2,2,64,512]{3,2,1,0:T(8,128)} %rs_hbm.1, f32[2,2,32,64]{3,2,1,0:T(8,128)} %d_hbm.1, f32[2,32,64]{2,1,0:T(8,128)} %bitcast.1), custom_call_target="tpu_custom_call" | custom-call | tf_op jit(solution)/shard_map/panels/pallas_call | solution.py:338
  66.6 0.7 %copy.7 = f32[2,2,32,512]{3,2,1,0:T(8,128)} copy(f32[2,2,32,512]{3,2,1,0:T(8,128)S(1)} %panels.1) | data formatting | bytes 524288

commit v3 on v2

--- a/solution.py
+++ b/solution.py
@@ -35,9 +35,8 @@
     return pl.ds(i * size if isinstance(i, int) else pl.multiple_of(i * size, size), size)
 
 
-def far_first(t):
-    half = (t + 1) // 2
-    return 8 + jnp.where(lax.rem(t, 2) == 1, -half, half)
+FAR_Z = (8, 7, 9, 6, 10, 5, 11, 4, 12, 3, 13, 2, 14, 1, 15)
+FAR_C = (10, 9, 11, 6, 14, 5, 7, 13, 15, 8, 2, 1, 3, 4, 12)
 
 
 def place(z):
@@ -46,7 +45,7 @@
 
 def kernel(
     s_hbm, u_hbm, rs_hbm, d_hbm, c_hbm, o_ref,
-    d_buf, c_buf, a_buf, s_buf, x_buf, pt, cx, p2, rb, rsb, rst, wh, wl, qa, cg, pu, ru, ug, ubh, ubl, pp, rc, ga, xb, xs, ob,
+    d_buf, c_buf, a_buf, s_buf, x_buf, pt, cx, p2, rb, ra, pm, rf, rsb, rst, wh, wl, qa, cg, pu, ru, ug, ubh, ubl, pp, rc, ga, xb, xs, ob,
     load_sem, zs, zr, cs, cr, ks, kr,
 ):
     row = lax.axis_index("row")
@@ -57,21 +56,20 @@
     def z_dev(i):
         return (lax.rem(z + i, NZ) * 2 + k, c)
 
+    def c_at(i):
+        return lax.rem(c // 4 + i // 4, 4) * 4 + lax.rem(c + i, 4)
+
     def c_dev(i):
-        return (row, lax.rem(c + i, NC))
+        return (row, c_at(i))
 
     sibling = (z * 2 + ok, c)
 
     barrier = pltpu.get_barrier_semaphore()
     pl.semaphore_signal(barrier, inc=1, device_id=sibling, device_id_type=MESH)
 
-    def greet(t, _):
-        i = far_first(t)
+    for i, j in zip(FAR_Z, FAR_C):
         pl.semaphore_signal(barrier, inc=1, device_id=z_dev(i), device_id_type=MESH)
-        pl.semaphore_signal(barrier, inc=1, device_id=c_dev(i), device_id_type=MESH)
-        return 0
-
-    lax.fori_loop(0, NZ - 1, greet, 0)
+        pl.semaphore_signal(barrier, inc=1, device_id=c_dev(j), device_id_type=MESH)
 
     def remote(src, dst, ssem, rsem, dev):
         return pltpu.make_async_remote_copy(
@@ -79,12 +77,8 @@
         )
 
     def z_send(g, src, dst):
-        def body(t, _):
-            i = far_first(t)
+        for i in FAR_Z:
             remote(src(lax.rem(z + i, NZ)), dst(z), zs.at[g, i], zr.at[g, i], z_dev(i)).start()
-            return 0
-
-        lax.fori_loop(0, NZ - 1, body, 0)
 
     def z_wait(g, i, src, dst):
         frm = lax.rem(z - i + NZ, NZ)
@@ -99,15 +93,11 @@
         lax.fori_loop(1, NZ, body, 0)
 
     def c_send(g, src, dst):
-        def body(t, _):
-            i = far_first(t)
-            remote(src(lax.rem(c + i, NC)), dst(c), cs.at[g, i], cr.at[g, i], c_dev(i)).start()
-            return 0
-
-        lax.fori_loop(0, NC - 1, body, 0)
+        for i in FAR_C:
+            remote(src(c_at(i)), dst(c), cs.at[g, i], cr.at[g, i], c_dev(i)).start()
 
     def c_wait(g, i, src, dst):
-        frm = lax.rem(c - i + NC, NC)
+        frm = lax.rem(c // 4 - i // 4 + 4, 4) * 4 + lax.rem(c - lax.rem(i, 4) + 4, 4)
         remote(src(frm), dst(frm), cs.at[g, i], cr.at[g, i], c_dev(i)).wait_recv()
         return frm
 
@@ -171,28 +161,48 @@
     own_ct = cg.at[tile(place(z), 32)]
     own_ct[...] = jnp.concatenate([c_buf[0], -c_buf[1]], 1)
 
-    pl.semaphore_wait(barrier, 1 + (NZ - 1) + (NC - 1))
-
     def cpl_copy(i):
         return remote(own_ct, own_ct, zs.at[Z_CPL, i], zr.at[Z_CPL, i], z_dev(i))
 
+    pl.semaphore_wait(barrier, 1 + (NZ - 1) + (NC - 1))
     for i in (8, 4, 12):
         cpl_copy(i).start()
-    own_d = d_buf.at[k]
-    k_copy(K_INV, own_d, own_d).start()
+
 
     for p in range(2):
         lo, mid, hi = p * 128, p * 128 + 64, p * 128 + 128
         re = x_buf[0, lo:mid] + x_buf[1, mid:hi]
         im = x_buf[1, lo:mid] - x_buf[0, mid:hi]
         pt[p] = jnp.concatenate([re, im], axis=0).T
+        rst[p] = rsb[p].T
+
+
+    for p in range(2):
         k_copy(K_PRIOR + p, pt.at[p, tile(ok, 256)], cx.at[p]).start()
+    own_d = d_buf.at[k]
+    k_copy(K_INV, own_d, own_d).start()
+
     for p in range(2):
         k_copy(K_PRIOR + p, pt.at[p, tile(ok, 256)], cx.at[p]).wait_recv()
-        p2[p] = pt[p, tile(k, 256)] + cx[p]
-        z_send(Z_PRIOR + p, lambda i: p2.at[p, tile(i, 16)], lambda i: rb.at[p, tile(i, 16)])
-    for p in range(2):
-        rst[p] = rsb[p].T
+        if p == 0:
+            p2[0] = pt[0, tile(k, 256)] + cx[0]
+            z_send(Z_PRIOR, lambda i: p2.at[0, tile(i, 16)], lambda i: rb.at[tile(i, 16)])
+    for i in range(NZ):
+        p2[1, tile(place(i), 16)] = pt[1, pl.ds(pl.multiple_of(k * 256 + i * 16, 16), 16)] + cx[1, tile(i, 16)]
+
+    near = ((0, 1, 0, 0, 64), (1, -1, 1, 0, 64), (2, 2, 2, 0, 32), (3, -2, 2, 32, 32))
+
+    def near_copy(n, step, to, first, rows):
+        group = lax.rem(z + step + NZ, 4)
+        src = p2.at[1, pl.ds(pl.multiple_of(group * 64 + first, 32), rows)]
+        return remote(src, ra.at[to, pl.ds(first, rows)], zs.at[1, n], zr.at[1, n], z_dev(step + NZ))
+
+    def fourth_copy(i):
+        src = pm.at[tile(lax.rem(z + i, NZ) // 4, 16)]
+        return remote(src, rf.at[i // 4], zs.at[1, i], zr.at[1, i], z_dev(i))
+
+    for args in near:
+        near_copy(*args).start()
     k_copy(K_INV, own_d, d_buf.at[ok]).wait_recv()
     at = lax.broadcasted_iota(jnp.int32, (32, 64), 0) - lax.broadcasted_iota(jnp.int32, (32, 64), 1)
     for p in range(2):
@@ -214,12 +224,24 @@
     for n, step, first, rows in onward:
         onward_copy(n, step, first, rows, z).start()
 
+    for args in near:
+        near_copy(*args).wait_recv()
+    pm[...] = p2[1, tile(lax.rem(z, 4), 64)] + ra[0] + (ra[1] + ra[2])
+    for i in (8, 4, 12):
+        fourth_copy(i).start()
+
     def gather_q(p):
         def arrived(i, total):
-            frm = z_wait(Z_PRIOR + p, i, lambda i: p2.at[p, tile(i, 16)], lambda i: rb.at[p, tile(i, 16)])
-            return total + rb[p, tile(frm, 16)]
-
-        total = lax.fori_loop(1, NZ, arrived, p2[p, tile(z, 16)])
+            frm = z_wait(Z_PRIOR, i, lambda i: p2.at[0, tile(i, 16)], lambda i: rb.at[tile(i, 16)])
+            return total + rb[tile(frm, 16)]
+
+        if p == 0:
+            total = lax.fori_loop(1, NZ, arrived, p2[0, tile(z, 16)])
+        else:
+            total = pm[tile(z // 4, 16)]
+            for i in (4, 8, 12):
+                fourth_copy(i).wait_recv()
+                total = total + rf[i // 4]
         own_q = qa.at[p, tile(z, 16)]
         own_q[...] = rst[p, tile(lax.rem(z, 8), 16)] - total
         z_send(Z_Q + p, lambda i: own_q, lambda i: qa.at[p, tile(i, 16)])
@@ -309,9 +331,9 @@
                 o_ref[s, p, :, pl.ds(h * 256, 256)] = turned[at : at + 32]
 
     def drain(i, _):
-        blk, big, act = rb.at[0, pl.ds(0, 16)], ru.at[pl.ds(0, 32)], ga.at[:, pl.ds(0, 128)]
+        blk, big, act = rb.at[pl.ds(0, 16)], ru.at[pl.ds(0, 32)], ga.at[:, pl.ds(0, 128)]
         q = qa.at[0, pl.ds(0, 16)]
-        for g, ref in ((0, blk), (1, blk), (3, q), (4, q), (5, act)):
+        for g, ref in ((0, blk), (3, q), (4, q), (5, act)):
             remote(ref, ref, zs.at[g, i], zr.at[g, i], z_dev(i)).wait_send()
         for g, ref in ((0, blk), (1, blk), (2, big), (3, big), (4, blk), (5, blk)):
             remote(ref, ref, cs.at[g, i], cr.at[g, i], c_dev(i)).wait_send()
@@ -320,6 +342,9 @@
     lax.fori_loop(1, NZ, drain, 0)
     for i in (4, 8, 12):
         cpl_copy(i).wait_send()
+        fourth_copy(i).wait_send()
+    for args in near:
+        near_copy(*args).wait_send()
     for n, step, first, rows in onward:
         onward_copy(n, step, first, rows, z).wait_send()
     k_copy(0, cx.at[0], cx.at[0]).wait_send()
@@ -342,7 +367,7 @@
         out_specs=vmem,
         scratch_shapes=[
             f(2, 2, 2, 32, 64), f(2, 32, 64), f(256, 1024), f(2, 1024, 512), f(2, 256, 512), f(2, 512, 128),
-            f(2, 256, 128), f(2, 256, 128), f(2, 256, 128), f(2, 128, 128), f(2, 128, 128),
+            f(2, 256, 128), f(2, 256, 128), f(256, 128), f(3, 64, 128), f(64, 128), f(4, 16, 128), f(2, 128, 128), f(2, 128, 128),
             b(2, 128, 128), b(2, 128, 128), f(2, 256, 128), f(512, 128), f(512, 128), f(512, 128), f(2, 512, 128),
             b(2048, 128), b(2048, 128), f(2, 256, 128), f(2, 256, 128), f(16, 2048), f(2, 16, 128), f(2, 16, 128),
             f(2, 256, 128),

time: 67.5 us -> 64.5 us (0.956)
  Pallas kernels: 66.6 us -> 63.6 us
    pallas_call x1, Pallas kernels: 66.6 us -> 63.6 us  [per_device(): pl.pallas_call(kernel, out_shape=pltpu.VMEM((2, 2, 32, 512), F32), in_spe...]
where the time goes in v3:
time: 64.5 us; the launch traced here: 64.4 us
  Pallas kernels  63.6 us (99%)
  local copies, waits for them, and re-layouts  0.71 us (1%)
    pallas_call x1, Pallas kernels, per_device(): pl.pallas_call(kernel, out_shape=pltpu.VMEM((2, 2, 32, 512), F32), in_spe...  63.6 us

profile of v3, /device:TPU:1, one launch (start us, length us, event | category | flops | bytes accessed | tf_op | source)
XLA Modules:
  0.0 64.4 jit_solution(8073736563459322924)
XLA Ops:
  0.0 63.6 %panels.1 = f32[2,2,32,512]{3,2,1,0:T(8,128)S(1)} custom-call(f32[2,1024,512]{2,1,0:T(8,128)} %s_hbm.1, f32[2,2,64,1024]{3,2,1,0:T(8,128)} %u_hbm.1, f32[2,2,64,512]{3,2,1,0:T(8,128)} %rs_hbm.1, f32[2,2,32,64]{3,2,1,0:T(8,128)} %d_hbm.1, f32[2,32,64]{2,1,0:T(8,128)} %bitcast.1), custom_call_target="tpu_custom_call" | custom-call | tf_op jit(solution)/shard_map/panels/pallas_call | solution.py:363
  63.7 0.7 %copy.7 = f32[2,2,32,512]{3,2,1,0:T(8,128)} copy(f32[2,2,32,512]{3,2,1,0:T(8,128)S(1)} %panels.1) | data formatting | bytes 524288

commit v4 on v3

--- a/solution.py
+++ b/solution.py
@@ -15,7 +15,7 @@
 KSTEP = 512
 VMEM = 62 * 1024 * 1024
 
-Z_PRIOR, Z_CPL, Z_Q, Z_ANS, Z_CPL2 = 0, 2, 3, 5, 6
+Z_PRIOR, Z_NEAR, Z_CPL, Z_Q, Z_ANS, Z_CPL2, Z_FOURTH = 0, 1, 2, 3, 5, 6, 7
 C_ANS, C_U, C_UALL, C_OUT = 0, 2, 3, 4
 K_PRIOR, K_INV, K_OUT, K_U = 0, 2, 3, 5
 
@@ -78,35 +78,23 @@
 
     def z_send(g, src, dst):
         for i in FAR_Z:
-            remote(src(lax.rem(z + i, NZ)), dst(z), zs.at[g, i], zr.at[g, i], z_dev(i)).start()
-
-    def z_wait(g, i, src, dst):
-        frm = lax.rem(z - i + NZ, NZ)
-        remote(src(frm), dst(frm), zs.at[g, i], zr.at[g, i], z_dev(i)).wait_recv()
-        return frm
-
-    def z_wait_all(g, src, dst):
-        def body(i, _):
-            z_wait(g, i, src, dst)
-            return 0
-
-        lax.fori_loop(1, NZ, body, 0)
+            remote(src(lax.rem(z + i, NZ)), dst(z), zs.at[g], zr.at[g], z_dev(i)).start()
+
+    def z_all(g, ref):
+        return remote(ref, ref, zs.at[g], zr.at[g], z_dev(1))
 
     def c_send(g, src, dst):
         for i in FAR_C:
-            remote(src(c_at(i)), dst(c), cs.at[g, i], cr.at[g, i], c_dev(i)).start()
-
-    def c_wait(g, i, src, dst):
-        frm = lax.rem(c // 4 - i // 4 + 4, 4) * 4 + lax.rem(c - lax.rem(i, 4) + 4, 4)
-        remote(src(frm), dst(frm), cs.at[g, i], cr.at[g, i], c_dev(i)).wait_recv()
-        return frm
-
-    def c_wait_all(g, src, dst):
-        def body(i, _):
-            c_wait(g, i, src, dst)
-            return 0
-
-        lax.fori_loop(1, NC, body, 0)
+            remote(src(c_at(i)), dst(c), cs.at[g], cr.at[g], c_dev(i)).start()
+
+    def c_all(g, ref):
+        return remote(ref, ref, cs.at[g], cr.at[g], c_dev(1))
+
+    def block_sum(ref, size):
+        parts = [ref[pl.ds(i * size, size)] for i in range(16)]
+        while len(parts) > 1:
+            parts = [one + two for one, two in zip(parts[::2], parts[1::2])]
+        return parts[0]
 
     def k_copy(g, src, dst):
         return remote(src, dst, ks.at[g], kr.at[g], sibling)
@@ -162,7 +150,7 @@
     own_ct[...] = jnp.concatenate([c_buf[0], -c_buf[1]], 1)
 
     def cpl_copy(i):
-        return remote(own_ct, own_ct, zs.at[Z_CPL, i], zr.at[Z_CPL, i], z_dev(i))
+        return remote(own_ct, own_ct, zs.at[Z_CPL], zr.at[Z_CPL], z_dev(i))
 
     pl.semaphore_wait(barrier, 1 + (NZ - 1) + (NC - 1))
     for i in (8, 4, 12):
@@ -195,11 +183,11 @@
     def near_copy(n, step, to, first, rows):
         group = lax.rem(z + step + NZ, 4)
         src = p2.at[1, pl.ds(pl.multiple_of(group * 64 + first, 32), rows)]
-        return remote(src, ra.at[to, pl.ds(first, rows)], zs.at[1, n], zr.at[1, n], z_dev(step + NZ))
+        return remote(src, ra.at[pl.ds(to * 64 + first, rows)], zs.at[Z_NEAR], zr.at[Z_NEAR], z_dev(step + NZ))
 
     def fourth_copy(i):
         src = pm.at[tile(lax.rem(z + i, NZ) // 4, 16)]
-        return remote(src, rf.at[i // 4], zs.at[1, i], zr.at[1, i], z_dev(i))
+        return remote(src, rf.at[i // 4], zs.at[Z_FOURTH], zr.at[Z_FOURTH], z_dev(i))
 
     for args in near:
         near_copy(*args).start()
@@ -217,54 +205,45 @@
 
     def onward_copy(n, step, first, rows, frm):
         ref = cg.at[pl.ds(pl.multiple_of(lax.rem(frm, 4) * 128 + first, 64), rows)]
-        return remote(ref, ref, zs.at[Z_CPL2, n], zr.at[Z_CPL2, n], z_dev(step + NZ))
-
-    for i in (4, 8, 12):
-        cpl_copy(i).wait_recv()
+        return remote(ref, ref, zs.at[Z_CPL2], zr.at[Z_CPL2], z_dev(step + NZ))
+
+    z_all(Z_CPL, cg.at[pl.ds(0, 96)]).wait_recv()
     for n, step, first, rows in onward:
         onward_copy(n, step, first, rows, z).start()
 
-    for args in near:
-        near_copy(*args).wait_recv()
-    pm[...] = p2[1, tile(lax.rem(z, 4), 64)] + ra[0] + (ra[1] + ra[2])
+    z_all(Z_NEAR, ra).wait_recv()
+    pm[...] = p2[1, tile(lax.rem(z, 4), 64)] + ra[0:64] + (ra[64:128] + ra[128:192])
     for i in (8, 4, 12):
         fourth_copy(i).start()
 
     def gather_q(p):
-        def arrived(i, total):
-            frm = z_wait(Z_PRIOR, i, lambda i: p2.at[0, tile(i, 16)], lambda i: rb.at[tile(i, 16)])
-            return total + rb[tile(frm, 16)]
-
         if p == 0:
-            total = lax.fori_loop(1, NZ, arrived, p2[0, tile(z, 16)])
+            rb[tile(z, 16)] = p2[0, tile(z, 16)]
+            z_all(Z_PRIOR, rb.at[pl.ds(0, 240)]).wait_recv()
+            total = block_sum(rb, 16)
         else:
-            total = pm[tile(z // 4, 16)]
-            for i in (4, 8, 12):
-                fourth_copy(i).wait_recv()
-                total = total + rf[i // 4]
+            z_all(Z_FOURTH, rf.at[pl.ds(1, 3)]).wait_recv()
+            total = pm[tile(z // 4, 16)] + rf[1] + (rf[2] + rf[3])
         own_q = qa.at[p, tile(z, 16)]
         own_q[...] = rst[p, tile(lax.rem(z, 8), 16)] - total
         z_send(Z_Q + p, lambda i: own_q, lambda i: qa.at[p, tile(i, 16)])
 
     gather_q(0)
 
-    for n, step, first, rows in onward:
-        onward_copy(n, step, first, rows, z - step + NZ).wait_recv()
+    z_all(Z_CPL2, cg.at[pl.ds(0, 384)]).wait_recv()
     pu[...] = dot3(split(cg[...]), (wh[1], wl[1]))
     c_send(C_U, lambda i: pu.at[tile(i, 32)], lambda i: ru.at[tile(i, 32)])
     gather_q(1)
 
     def lower(p):
-        z_wait_all(Z_Q + p, lambda i: qa.at[p, tile(z, 16)], lambda i: qa.at[p, tile(i, 16)])
+        z_all(Z_Q + p, qa.at[p, pl.ds(0, 240)]).wait_recv()
         pp[p] = dot3(split(qa[p]), (wh[p], wl[p]))
         c_send(C_ANS + p, lambda i: pp.at[p, tile(i, 16)], lambda i: rc.at[p, tile(i, 16)])
 
     def summed(p):
-        def arrived(i, total):
-            frm = c_wait(C_ANS + p, i, lambda i: pp.at[p, tile(i, 16)], lambda i: rc.at[p, tile(i, 16)])
-            return total + rc[p, tile(frm, 16)]
-
-        return lax.fori_loop(1, NC, arrived, pp[p, tile(c, 16)])
+        rc[p, tile(c, 16)] = pp[p, tile(c, 16)]
+        c_all(C_ANS + p, rc.at[p, pl.ds(0, 240)]).wait_recv()
+        return block_sum(rc.at[p], 16)
 
     lane = lax.broadcasted_iota(jnp.int32, (16, 128), 1)
     own_lanes = lane // 64 == k
@@ -280,12 +259,10 @@
 
     lower(0)
 
-    def u_arrived(i, total):
-        frm = c_wait(C_U, i, lambda i: pu.at[tile(i, 32)], lambda i: ru.at[tile(i, 32)])
-        return total + ru[tile(frm, 32)]
-
+    ru[tile(c, 32)] = pu[tile(c, 32)]
+    c_all(C_U, ru.at[pl.ds(0, 480)]).wait_recv()
     own_u = ug.at[k, tile(c, 32)]
-    own_u[...] = lax.fori_loop(1, NC, u_arrived, pu[tile(c, 32)])
+    own_u[...] = block_sum(ru, 32)
     c_send(C_UALL, lambda i: own_u, lambda i: ug.at[k, tile(i, 32)])
 
     own_a = ga.at[:, tile(z, 128)]
@@ -297,7 +274,7 @@
 
     lower(1)
 
-    c_wait_all(C_UALL, lambda i: own_u, lambda i: ug.at[k, tile(i, 32)])
+    c_all(C_UALL, ug.at[k, pl.ds(0, 480)]).wait_recv()
     half = ug.at[k]
     k_copy(K_U, half, half).start()
     share(0)
@@ -317,36 +294,31 @@
     lax.fori_loop(0, NC, weigh, 0)
     own_1 = summed(1)
 
-    z_wait_all(Z_ANS, lambda i: own_a, lambda i: ga.at[:, tile(i, 128)])
+    z_all(Z_ANS, ga.at[:, pl.ds(0, 15 * 128)]).wait_recv()
     xb[1] = own_1 - dot3(split(ga[...]), (ubh[...], ubl[...]))
     swap(1).start()
     share(1)
 
     for p in range(2):
-        c_wait_all(C_OUT + p, lambda i: ob.at[p, tile(c, 16)], lambda i: ob.at[p, tile(i, 16)])
+        c_all(C_OUT + p, ob.at[p, pl.ds(0, 240)]).wait_recv()
         turned = ob[p].T
         for h in range(2):
             for s in range(2):
                 at = (h * 2 + s) * 32
                 o_ref[s, p, :, pl.ds(h * 256, 256)] = turned[at : at + 32]
 
-    def drain(i, _):
-        blk, big, act = rb.at[pl.ds(0, 16)], ru.at[pl.ds(0, 32)], ga.at[:, pl.ds(0, 128)]
-        q = qa.at[0, pl.ds(0, 16)]
-        for g, ref in ((0, blk), (3, q), (4, q), (5, act)):
-            remote(ref, ref, zs.at[g, i], zr.at[g, i], z_dev(i)).wait_send()
-        for g, ref in ((0, blk), (1, blk), (2, big), (3, big), (4, blk), (5, blk)):
-            remote(ref, ref, cs.at[g, i], cr.at[g, i], c_dev(i)).wait_send()
-        return 0
-
-    lax.fori_loop(1, NZ, drain, 0)
-    for i in (4, 8, 12):
-        cpl_copy(i).wait_send()
-        fourth_copy(i).wait_send()
-    for args in near:
-        near_copy(*args).wait_send()
-    for n, step, first, rows in onward:
-        onward_copy(n, step, first, rows, z).wait_send()
+    z_all(Z_PRIOR, rb.at[pl.ds(0, 240)]).wait_send()
+    z_all(Z_NEAR, ra).wait_send()
+    z_all(Z_CPL, cg.at[pl.ds(0, 96)]).wait_send()
+    z_all(Z_CPL2, cg.at[pl.ds(0, 384)]).wait_send()
+    z_all(Z_FOURTH, rf.at[pl.ds(1, 3)]).wait_send()
+    z_all(Z_ANS, ga.at[:, pl.ds(0, 15 * 128)]).wait_send()
+    c_all(C_U, ru.at[pl.ds(0, 480)]).wait_send()
+    c_all(C_UALL, ug.at[k, pl.ds(0, 480)]).wait_send()
+    for p in range(2):
+        z_all(Z_Q + p, qa.at[p, pl.ds(0, 240)]).wait_send()
+        c_all(C_ANS + p, rc.at[p, pl.ds(0, 240)]).wait_send()
+        c_all(C_OUT + p, ob.at[p, pl.ds(0, 240)]).wait_send()
     k_copy(0, cx.at[0], cx.at[0]).wait_send()
     k_copy(1, cx.at[1], cx.at[1]).wait_send()
     k_copy(K_INV, own_d, own_d).wait_send()
@@ -367,13 +339,13 @@
         out_specs=vmem,
         scratch_shapes=[
             f(2, 2, 2, 32, 64), f(2, 32, 64), f(256, 1024), f(2, 1024, 512), f(2, 256, 512), f(2, 512, 128),
-            f(2, 256, 128), f(2, 256, 128), f(256, 128), f(3, 64, 128), f(64, 128), f(4, 16, 128), f(2, 128, 128), f(2, 128, 128),
+            f(2, 256, 128), f(2, 256, 128), f(256, 128), f(192, 128), f(64, 128), f(4, 16, 128), f(2, 128, 128), f(2, 128, 128),
             b(2, 128, 128), b(2, 128, 128), f(2, 256, 128), f(512, 128), f(512, 128), f(512, 128), f(2, 512, 128),
             b(2048, 128), b(2048, 128), f(2, 256, 128), f(2, 256, 128), f(16, 2048), f(2, 16, 128), f(2, 16, 128),
             f(2, 256, 128),
             pltpu.SemaphoreType.DMA((18,)),
-            pltpu.SemaphoreType.DMA((7, 16)), pltpu.SemaphoreType.DMA((7, 16)),
-            pltpu.SemaphoreType.DMA((6, 16)), pltpu.SemaphoreType.DMA((6, 16)),
+            pltpu.SemaphoreType.DMA((8,)), pltpu.SemaphoreType.DMA((8,)),
+            pltpu.SemaphoreType.DMA((6,)), pltpu.SemaphoreType.DMA((6,)),
             pltpu.SemaphoreType.DMA((6,)), pltpu.SemaphoreType.DMA((6,)),
         ],
         compiler_params=pltpu.CompilerParams(

time: 64.5 us -> 60.7 us (0.941)
  Pallas kernels: 63.6 us -> 59.9 us
    pallas_call x1, Pallas kernels: 63.6 us -> 59.9 us  [per_device(): pl.pallas_call(kernel, out_shape=pltpu.VMEM((2, 2, 32, 512), F32), in_spe...]
where the time goes in v4:
time: 60.7 us; the launch traced here: 60.6 us
  Pallas kernels  59.9 us (99%)
  local copies, waits for them, and re-layouts  0.71 us (1%)
    pallas_call x1, Pallas kernels, per_device(): pl.pallas_call(kernel, out_shape=pltpu.VMEM((2, 2, 32, 512), F32), in_spe...  59.9 us

profile of v4, /device:TPU:1, one launch (start us, length us, event | category | flops | bytes accessed | tf_op | source)
XLA Modules:
  0.0 60.6 jit_solution(13410943212633609434)
XLA Ops:
  0.0 59.9 %panels.1 = f32[2,2,32,512]{3,2,1,0:T(8,128)S(1)} custom-call(f32[2,1024,512]{2,1,0:T(8,128)} %s_hbm.1, f32[2,2,64,1024]{3,2,1,0:T(8,128)} %u_hbm.1, f32[2,2,64,512]{3,2,1,0:T(8,128)} %rs_hbm.1, f32[2,2,32,64]{3,2,1,0:T(8,128)} %d_hbm.1, f32[2,32,64]{2,1,0:T(8,128)} %bitcast.1), custom_call_target="tpu_custom_call" | custom-call | tf_op jit(solution)/shard_map/panels/pallas_call | solution.py:335
  59.9 0.7 %copy.7 = f32[2,2,32,512]{3,2,1,0:T(8,128)} copy(f32[2,2,32,512]{3,2,1,0:T(8,128)S(1)} %panels.1) | data formatting | bytes 524288

commit v5 on v4

--- a/solution.py
+++ b/solution.py
@@ -152,10 +152,6 @@
     def cpl_copy(i):
         return remote(own_ct, own_ct, zs.at[Z_CPL], zr.at[Z_CPL], z_dev(i))
 
-    pl.semaphore_wait(barrier, 1 + (NZ - 1) + (NC - 1))
-    for i in (8, 4, 12):
-        cpl_copy(i).start()
-
 
     for p in range(2):
         lo, mid, hi = p * 128, p * 128 + 64, p * 128 + 128
@@ -165,6 +161,9 @@
         rst[p] = rsb[p].T
 
 
+    pl.semaphore_wait(barrier, 1 + (NZ - 1) + (NC - 1))
+    for i in (8, 4, 12):
+        cpl_copy(i).start()
     for p in range(2):
         k_copy(K_PRIOR + p, pt.at[p, tile(ok, 256)], cx.at[p]).start()
     own_d = d_buf.at[k]
@@ -174,7 +173,6 @@
         k_copy(K_PRIOR + p, pt.at[p, tile(ok, 256)], cx.at[p]).wait_recv()
         if p == 0:
             p2[0] = pt[0, tile(k, 256)] + cx[0]
-            z_send(Z_PRIOR, lambda i: p2.at[0, tile(i, 16)], lambda i: rb.at[tile(i, 16)])
     for i in range(NZ):
         p2[1, tile(place(i), 16)] = pt[1, pl.ds(pl.multiple_of(k * 256 + i * 16, 16), 16)] + cx[1, tile(i, 16)]
 
@@ -191,6 +189,7 @@
 
     for args in near:
         near_copy(*args).start()
+    z_send(Z_PRIOR, lambda i: p2.at[0, tile(i, 16)], lambda i: rb.at[tile(i, 16)])
     k_copy(K_INV, own_d, d_buf.at[ok]).wait_recv()
     at = lax.broadcasted_iota(jnp.int32, (32, 64), 0) - lax.broadcasted_iota(jnp.int32, (32, 64), 1)
     for p in range(2):
@@ -272,11 +271,11 @@
     xb[0] = answer_0
     swap(0).start()
 
-    lower(1)
-
     c_all(C_UALL, ug.at[k, pl.ds(0, 480)]).wait_recv()
     half = ug.at[k]
     k_copy(K_U, half, half).start()
+    lower(1)
+
     share(0)
 
     k_copy(K_U, half, ug.at[ok]).wait_recv()

time: 60.7 us -> 60.3 us (level)
  no operation moved by 1% of the time
where the time goes in v5:
time: 60.3 us; the launch traced here: 60.2 us
  Pallas kernels  59.5 us (99%)
  local copies, waits for them, and re-layouts  0.71 us (1%)
    pallas_call x1, Pallas kernels, per_device(): pl.pallas_call(kernel, out_shape=pltpu.VMEM((2, 2, 32, 512), F32), in_spe...  59.5 us

profile of v5, /device:TPU:1, one launch (start us, length us, event | category | flops | bytes accessed | tf_op | source)
XLA Modules:
  0.0 60.2 jit_solution(2827533368725703706)
XLA Ops:
  0.0 59.5 %panels.1 = f32[2,2,32,512]{3,2,1,0:T(8,128)S(1)} custom-call(f32[2,1024,512]{2,1,0:T(8,128)} %s_hbm.1, f32[2,2,64,1024]{3,2,1,0:T(8,128)} %u_hbm.1, f32[2,2,64,512]{3,2,1,0:T(8,128)} %rs_hbm.1, f32[2,2,32,64]{3,2,1,0:T(8,128)} %d_hbm.1, f32[2,32,64]{2,1,0:T(8,128)} %bitcast.1), custom_call_target="tpu_custom_call" | custom-call | tf_op jit(solution)/shard_map/panels/pallas_call | solution.py:334
  59.5 0.7 %copy.7 = f32[2,2,32,512]{3,2,1,0:T(8,128)} copy(f32[2,2,32,512]{3,2,1,0:T(8,128)S(1)} %panels.1) | data formatting | bytes 524288

commit v6 on v5

--- a/solution.py
+++ b/solution.py
@@ -294,7 +294,9 @@
     own_1 = summed(1)
 
     z_all(Z_ANS, ga.at[:, pl.ds(0, 15 * 128)]).wait_recv()
-    xb[1] = own_1 - dot3(split(ga[...]), (ubh[...], ubl[...]))
+    hi, lo = split(ga[...])
+    first = jnp.dot(jnp.concatenate([hi, lo], 0), ubh[...], preferred_element_type=F32)
+    xb[1] = own_1 - (first[:16] + (first[16:] + jnp.dot(hi, ubl[...], preferred_element_type=F32)))
     swap(1).start()
     share(1)
 

time: 60.3 us -> 60.3 us (level)
  no operation moved by 1% of the time
where the time goes in v6:
time: 60.3 us; the launch traced here: 60.2 us
  Pallas kernels  59.5 us (99%)
  local copies, waits for them, and re-layouts  0.71 us (1%)
    pallas_call x1, Pallas kernels, per_device(): pl.pallas_call(kernel, out_shape=pltpu.VMEM((2, 2, 32, 512), F32), in_spe...  59.5 us

profile of v6, /device:TPU:1, one launch (start us, length us, event | category | flops | bytes accessed | tf_op | source)
XLA Modules:
  0.0 60.2 jit_solution(15046430440234570331)
XLA Ops:
  0.0 59.5 %panels.1 = f32[2,2,32,512]{3,2,1,0:T(8,128)S(1)} custom-call(f32[2,1024,512]{2,1,0:T(8,128)} %s_hbm.1, f32[2,2,64,1024]{3,2,1,0:T(8,128)} %u_hbm.1, f32[2,2,64,512]{3,2,1,0:T(8,128)} %rs_hbm.1, f32[2,2,32,64]{3,2,1,0:T(8,128)} %d_hbm.1, f32[2,32,64]{2,1,0:T(8,128)} %bitcast.1), custom_call_target="tpu_custom_call" | custom-call | tf_op jit(solution)/shard_map/panels/pallas_call | solution.py:336
  59.5 0.7 %copy.7 = f32[2,2,32,512]{3,2,1,0:T(8,128)} copy(f32[2,2,32,512]{3,2,1,0:T(8,128)S(1)} %panels.1) | data formatting | bytes 524288
